TPU v7x, 32 devices: a whole 2x2x4 slice. The times are simulated.
32 devices in a mesh: gx: 4 (over z), gy: 8 (over y, x, core).
Axes of the slice: x: 2, y: 2, z: 4, core: 2. Of those that a mesh axis runs over, the one named last changes fastest.
Arguments:
- right_side: float32 [128, 256, 128], P('gx', 'gy'), may hold values from -6 to 6
- permittivity: float32 [128, 256, 128], P('gx', 'gy'), may hold values from 0.175 to 5.6
Outputs:
- potential: float32 [128, 256, 128], P('gx', 'gy')
All inputs are finite; a program needn't handle non-finite values.
Results may differ from a plain program's by a relative error of at most 0.00002.
Values sent between devices are 32-bit elements; how exact they have to be, the bound alone decides.
A program may use at most 192 MiB of HBM per device.

v0:
```python
import functools

import jax
import jax.numpy as jnp
from jax import lax
from jax.experimental import pallas as pl
from jax.experimental.pallas import tpu as pltpu
from jax.sharding import PartitionSpec as P

LEVELS = 5
SMOOTH = 2
COARSE_SWEEPS = 12
MESH = pl.DeviceIdType.MESH
F32 = jnp.float32


DIRS = [(dx, dy) for dx in (-1, 0, 1) for dy in (-1, 0, 1) if (dx, dy) != (0, 0)]
DIRS.sort(key=lambda d: (d[0] == 0, d[1] != 0))


class Level:
    pass


def iota(shape, dim):
    return lax.broadcasted_iota(jnp.int32, shape, dim)


def even_mask(rows, lanes):
    return (iota((rows, lanes), 0) + iota((rows, lanes), 1)) % 2 == 0


def roll(x, shift, axis):
    return pltpu.roll(x, shift % x.shape[axis], axis)


def sum_lanes(x, lanes):
    pick = jnp.where(iota((lanes, lanes), 0) // 2 == iota((lanes, lanes), 1), F32(0.125), F32(0.0))
    return jnp.dot(x, pick, precision=lax.Precision.HIGHEST, preferred_element_type=F32)


def spread_lanes(x, lanes):
    pick = jnp.where(iota((lanes, lanes), 0) == iota((lanes, lanes), 1) // 2, F32(1.0), F32(0.0))
    return jnp.dot(x, pick, precision=lax.Precision.HIGHEST, preferred_element_type=F32)


def put_rows(tmp, t, values):
    for h in range(tmp.shape[1]):
        tmp[t, h, 0 : values.shape[-2], :] = values[..., h * 128 : h * 128 + 128]


def get_row(tmp, t, high):
    tiles = [tmp[t, h, 0:high, :] for h in range(tmp.shape[1])]
    return tiles[0] if len(tiles) == 1 else jnp.concatenate(tiles, axis=-1)


def get_strided(tmp, rows, count, first):
    tiles = [tmp[0:rows, h, pl.ds(first, count, 2), :] for h in range(tmp.shape[1])]
    return tiles[0] if len(tiles) == 1 else jnp.concatenate(tiles, axis=-1)


def restrict(tmp, rows, high):
    lanes = tmp.shape[1] * 128
    both = get_strided(tmp, rows, high // 2, 0) + get_strided(tmp, rows, high // 2, 1)
    flat = both.reshape(rows * (high // 2), lanes)
    return sum_lanes(flat, lanes).reshape(rows, high // 2, lanes)


def spread(tmp, coarse):
    rows, high, lanes = coarse.shape
    wide = spread_lanes(coarse.reshape(rows * high, lanes), lanes).reshape(rows, high, lanes)
    for h in range(tmp.shape[1]):
        part = wide[..., h * 128 : h * 128 + 128]
        tmp[0:rows, h, pl.ds(0, high, 2), :] = part
        tmp[0:rows, h, pl.ds(1, high, 2), :] = part


def wrap(level, ref):
    if level.whole:
        ref[0] = roll(ref[level.pairs], level.zlen, 1)
        ref[level.pairs + 1] = roll(ref[1], -level.zlen, 1)


def inverse(x):
    y = pl.reciprocal(x, approx=True)
    y = y * (2.0 - x * y)
    return y * (2.0 - x * y)


def loop(level, lo, hi, body):
    size = min(hi - lo, max(1, 32 * 1024 // (level.high * level.lanes)))
    if size < 1:
        return
    full = (hi - lo) // size

    def step(i, _):
        for k in range(size):
            body(lo + i * size + k)
        return 0

    if full > 1:
        lax.fori_loop(0, full, step, 0)
    else:
        step(0, 0)
    for t in range(lo + full * size, hi):
        body(t)


def reach(level, cells):
    if level.whole:
        return 0, level.pairs
    more = (cells + 1) // 2
    return level.rim_pairs - more, level.rim_pairs + level.block_pairs + more


def pack(level, get, put, lo, hi):
    s = even_mask(level.high, level.lanes)

    def step(t):
        first, second = get(2 * t), get(2 * t + 1)
        put(t, jnp.where(s, first, second), jnp.where(s, second, first))

    loop(level, lo, hi, step)


def put_e(level):
    def put(t, first, second):
        level.e[0][t + 1] = first
        level.e[1][t + 1] = second

    return put


class Ends:
    def __init__(self, level):
        shape = (level.high, level.lanes)
        row, lane = iota(shape, 0), iota(shape, 1)
        self.level = level
        self.s = even_mask(*shape)
        self.low_y, self.top_y = row == level.first_y, row == level.last_y
        self.low_z = lane % level.zlen == 0
        self.top_z = lane % level.zlen == level.zlen - 1
        if level.whole:
            self.low_x = lane < level.zlen
            self.top_x = (lane >= (level.gx - 1) * level.zlen) & (lane < level.gx * level.zlen)

    def beyond(self, c, t):
        level = self.level
        even = self.s if c == 0 else ~self.s
        at_low = jnp.asarray(t == level.first_x).astype(jnp.int32)
        at_top = jnp.asarray(t == level.last_x).astype(jnp.int32)
        out = jnp.where(even, at_low, at_top) > 0
        if level.whole:
            out = out & ((even & self.low_x) | (~even & self.top_x))
        return out


def finish(level, ends, c, t, w, beyond):
    total = ((w[0] + w[1]) + (w[2] + w[3])) + (w[4] + w[5])
    inv = inverse(total)
    level.inv[c, t] = inv
    w = list(w)
    w[1] = jnp.where(beyond, 0.0, w[1])
    w[2] = jnp.where(ends.top_y, 0.0, w[2])
    w[3] = jnp.where(ends.low_y, 0.0, w[3])
    for k in range(6):
        level.a[c, k, t] = w[k] * inv


def red_weights(level, ends, lo, hi):
    scale = F32(2.0 * 0.25**level.index)
    end_scale = F32(0.25**level.index)
    s = ends.s

    def step(t):
        own, other = level.e[0][t + 1], level.e[1][t + 1]
        outer = jnp.where(s, level.e[1][t], level.e[1][t + 2])
        scaled, end = scale * own, end_scale * own
        beyond = ends.beyond(0, t)

        def weight(n):
            return scaled * n * inverse(own + n)

        w = [
            weight(other),
            weight(outer),
            weight(roll(other, -1, 0)),
            weight(roll(other, 1, 0)),
            jnp.where(ends.top_z, 0.0, weight(roll(other, -1, 1))),
            jnp.where(ends.low_z, 0.0, weight(roll(other, 1, 1))),
        ]
        level.v[0][t + 1] = w[1]
        level.a[1, 0, t] = w[0]
        level.a[1, 2, t] = roll(w[3], -1, 0)
        level.a[1, 3, t] = roll(w[2], 1, 0)
        level.a[1, 4, t] = roll(w[5], -1, 1)
        level.a[1, 5, t] = roll(w[4], 1, 1)
        w[1] = jnp.where(beyond, end, w[1])
        w[2] = jnp.where(ends.top_y, end, w[2])
        w[3] = jnp.where(ends.low_y, end, w[3])
        finish(level, ends, 0, t, w, beyond)

    lax.fori_loop(lo, hi, lambda t, c: (step(t), c)[1], 0)


def black_weights(level, ends, lo, hi):
    end_scale = F32(0.25**level.index)

    def step(t):
        end = end_scale * level.e[1][t + 1]
        beyond = ends.beyond(1, t)
        w = [level.a[1, k, t] for k in (0, 0, 2, 3, 4, 5)]
        w[1] = jnp.where(ends.s, level.v[0][t + 2], level.v[0][t])
        w[1] = jnp.where(beyond, end, w[1])
        w[2] = jnp.where(ends.top_y, end, w[2])
        w[3] = jnp.where(ends.low_y, end, w[3])
        finish(level, ends, 1, t, w, beyond)

    lax.fori_loop(lo, hi, lambda t, c: (step(t), c)[1], 0)


def coefficients(level, cells):
    ends = Ends(level)
    lo, hi = reach(level, cells)
    more = 0 if level.whole else 1
    red_weights(level, ends, lo - more, hi + more)
    wrap(level, level.v[0])
    black_weights(level, ends, lo, hi)


def updated(level, c, t, s):
    v, a = level.v[1 - c], level.a
    other = v[t + 1]
    even = s if c == 0 else ~s
    outer = jnp.where(even, v[t], v[t + 2])
    x = level.e[c][t + 1] + a[c, 0, t] * other + a[c, 1, t] * outer
    y = a[c, 2, t] * roll(other, -1, 0) + a[c, 3, t] * roll(other, 1, 0)
    z = a[c, 4, t] * roll(other, -1, 1) + a[c, 5, t] * roll(other, 1, 1)
    return x + (y + z)


def half_sweep(level, c, cells):
    s = even_mask(level.high, level.lanes)

    def step(t):
        level.v[c][t + 1] = updated(level, c, t, s)

    loop(level, *reach(level, cells), step)
    wrap(level, level.v[c])


def sweeps(level, count, cells):
    for k in range(2 * count):
        half_sweep(level, k % 2, cells + 2 * count - 1 - k)


def start(level, get, cells, keep):
    def put(t, first, second):
        red = first * level.inv[0, t]
        level.e[0][t + 1] = red
        level.v[0][t + 1] = red
        level.e[1][t + 1] = second * level.inv[1, t]

    pack(level, get, put, *reach(level, keep))
    wrap(level, level.v[0])
    if cells is not None:
        half_sweep(level, 1, cells)


def solve_small(level, count):
    s = even_mask(level.high, level.lanes)
    a = [[level.a[c, k, 0] for k in range(6)] for c in range(2)]
    f = [level.e[c][1] for c in range(2)]

    def half(c, other):
        even = s if c == 0 else ~s
        outer = jnp.where(even, roll(other, level.zlen, 1), roll(other, -level.zlen, 1))
        x = f[c] + a[c][0] * other + a[c][1] * outer
        y = a[c][2] * roll(other, -1, 0) + a[c][3] * roll(other, 1, 0)
        z = a[c][4] * roll(other, -1, 1) + a[c][5] * roll(other, 1, 1)
        return x + (y + z)

    def step(_, v):
        red = half(0, v[1])
        return red, half(1, red)

    first = f[0]
    v = lax.fori_loop(0, count - 1, step, (first, half(1, first)))
    for c in range(2):
        level.v[c][1] = v[c]


def residual_sums(level, tmp):
    s = even_mask(level.high, level.lanes)
    lo, hi = reach(level, 0)
    ylo, high = level.rim_y, level.block_y

    def step(t):
        r = (updated(level, 0, t, s) - level.v[0][t + 1]) * inverse(level.inv[0, t])
        put_rows(tmp, t - lo, r[ylo : ylo + high])

    loop(level, lo, hi, step)


def coarse_row(level, s, x):
    red, black = level.v[0][x // 2 + 1], level.v[1][x // 2 + 1]
    return jnp.where(s, red, black) if x % 2 == 0 else jnp.where(s, black, red)


def kernel(gx, gy, right_ref, permit_ref, out_ref, refs, lv):
    me_x, me_y = lax.axis_index("gx"), lax.axis_index("gy")
    me = me_x * gy + me_y
    n = gx * gy
    l0, l1, l2, l3, l4 = lv
    send_sem, recv_sem, all_send, all_recv = refs["sems"]

    def inside(dx, dy):
        x, y = me_x + dx, me_y + dy
        return (x >= 0) & (x < gx) & (y >= 0) & (y < gy)

    def cut(d, size, rim, block):
        if d == 0:
            return pl.ds(rim, block), pl.ds(rim, block)
        if d == 1:
            return pl.ds(rim + block - size, size), pl.ds(rim - size, size)
        return pl.ds(rim, size), pl.ds(rim + block, size)

    def copies(kind, src, dst, width, geometry):
        rim_x, block_x, rim_y, block_y = geometry
        out = []
        for k, (dx, dy) in enumerate(DIRS):
            sx, tx = cut(dx, width, rim_x, block_x)
            sy, ty = cut(dy, 8, rim_y, block_y)
            copy = pltpu.make_async_remote_copy(
                src_ref=src.at[sx, sy],
                dst_ref=dst.at[tx, ty],
                send_sem=send_sem.at[kind, k],
                recv_sem=recv_sem.at[kind, k],
                device_id=(me_x + dx, me_y + dy),
                device_id_type=MESH,
            )
            out.append((dx, dy, copy))
        return out

    def go(group):
        for dx, dy, copy in group:
            pl.when(inside(dx, dy))(copy.start)

    def arrive(group):
        for dx, dy, copy in group:
            pl.when(inside(-dx, -dy))(copy.wait_recv)

    def sent(group):
        for dx, dy, copy in group:
            pl.when(inside(dx, dy))(copy.wait_send)

    e0, f0, e1, f1 = refs["e0"], refs["f0"], refs["e1"], refs["f1"]
    vh0, vh1 = refs["vh0"], refs["vh1"]
    g0, g1 = (l0.rim_x, l0.block_x, l0.rim_y, l0.block_y), (l1.rim_x, l1.block_x, l1.rim_y, l1.block_y)
    p0, p1 = (l0.rim_pairs + 1, l0.block_pairs) + g0[2:], (l1.rim_pairs + 1, l1.block_pairs) + g1[2:]
    deep = 2 * SMOOTH
    send_e0 = copies(0, e0, e0, deep + 1, g0)
    send_f0 = copies(1, f0, f0, deep, g0)
    send_e1 = copies(2, e1, e1, deep + 2, g1)
    send_f1 = copies(3, f1, f1, deep + 1, g1)
    send_v0, send_v1 = [], []
    for c in range(2):
        send_v0 += copies(4 + c, l0.v[c], vh0.at[c], deep // 2, p0)
        send_v1 += copies(6 + c, l1.v[c], vh1.at[c], deep // 2 + 1, p1)

    def fill(ref, lead, value, geometry):
        rim_x, block_x, rim_y, block_y = geometry
        rows, high, width = ref.shape[-3:]
        top_x, top_y = rim_x + block_x, rim_y + block_y
        for xs, ys in (
            ((0, rim_x), (0, high)),
            ((top_x, rows), (0, high)),
            ((rim_x, top_x), (0, rim_y)),
            ((rim_x, top_x), (top_y, high)),
        ):
            part = jnp.full((xs[1] - xs[0], ys[1] - ys[0], width), value, F32)
            ref[lead + (slice(*xs), slice(*ys))] = part

    fill(e0, (), 1.0, g0)
    fill(f0, (), 0.0, g0)
    fill(e1, (), 1.0, g1)
    fill(f1, (), 0.0, g1)
    for c in range(2):
        fill(vh0, (c,), 0.0, p0)
        fill(vh1, (c,), 0.0, p1)
    x0, y0 = pl.ds(l0.rim_x, l0.block_x), pl.ds(l0.rim_y, l0.block_y)
    e0[x0, y0, :] = permit_ref[...]
    f0[x0, y0, :] = right_ref[...]

    barrier = pltpu.get_barrier_semaphore()

    def device(d):
        t = lax.rem(me + d, n)
        return (lax.div(t, gy), lax.rem(t, gy))

    def greet(d, _):
        pl.semaphore_signal(barrier, inc=1, device_id=device(d), device_id_type=MESH)
        return 0

    lax.fori_loop(1, n, greet, 0)
    for level in (l0, l1):
        for c in range(2):
            for t in list(range(3)) + list(range(level.pairs - 1, level.pairs + 2)):
                level.v[c][t] = jnp.zeros((level.high, level.lanes), F32)
            for t in (0, level.pairs + 1):
                level.e[c][t] = jnp.ones((level.high, level.lanes), F32)
    pl.semaphore_wait(barrier, n - 1)

    go(send_e0)
    go(send_f0)

    tmp = refs["tmp"]
    lanes = l0.lanes

    def narrow(values, used, other):
        lane = iota(values.shape, len(values.shape) - 1)
        return jnp.where(lane < used, values, F32(other))

    put_rows(
        tmp,
        pl.ds(0, l1.block_x),
        permit_ref[...].reshape(l1.block_x, 2, l0.block_y, lanes).sum(axis=1),
    )
    own_e1 = narrow(restrict(tmp, l1.block_x, l0.block_y), l1.zlen, 1.0)
    e1[pl.ds(l1.rim_x, l1.block_x), pl.ds(l1.rim_y, l1.block_y), :] = own_e1
    go(send_e1)

    block2, z2 = l2.block_x, l2.zlen
    per = 128 // z2
    groups = block2 // per

    def gather_start(kind, rows):
        stage, packed = refs["stage"].at[kind], refs["packed"].at[kind]
        group = iota((8, 128), 1) // z2
        for g in range(groups):
            value = rows[g * per]
            for k in range(1, per):
                value = jnp.where(group == k, roll(rows[g * per + k], k * z2, 1), value)
            packed[g] = value
            stage[me, g] = value

        def step(d, _):
            pltpu.make_async_remote_copy(
                src_ref=packed,
                dst_ref=stage.at[me],
                send_sem=all_send.at[kind],
                recv_sem=all_recv.at[kind],
                device_id=device(d),
                device_id_type=MESH,
            ).start()
            return 0

        lax.fori_loop(1, n, step, 0)

    def gather_wait(kind, full):
        stage = refs["stage"].at[kind]
        others = stage.at[pl.ds(0, n - 1)]
        pltpu.make_async_copy(others, others, all_recv.at[kind]).wait()
        group = iota((8, 128), 1) // z2

        def step(q, _):
            for x in range(block2):
                tiles = []
                for h in range(full.shape[-1] // 128):
                    value = None
                    for k in range(per):
                        p = h * per + k
                        if p >= gx:
                            break
                        part = roll(stage[p * gy + q, x // per], (k - x % per) * z2, 1)
                        value = part if k == 0 else jnp.where(group == k, part, value)
                    tiles.append(value)
                row = tiles[0] if len(tiles) == 1 else jnp.concatenate(tiles, axis=1)
                full[x, pl.ds(pl.multiple_of(q * 8 + 8, 8), 8), :] = row
            return 0

        lax.fori_loop(0, gy, step, 0)

    def gather_end(kind):
        others = refs["stage"].at[kind, pl.ds(0, n - 1)]
        pltpu.make_async_copy(others, others, all_send.at[kind]).wait()

    put_rows(tmp, pl.ds(0, block2), own_e1.reshape(block2, 2, l1.block_y, lanes).sum(axis=1))
    gather_start(0, restrict(tmp, block2, l1.block_y))

    arrive([item for item in send_e0 if item[0] == 0])
    lo, hi = reach(l0, 0)
    ends = Ends(l0)
    pack(l0, lambda x: e0[x], put_e(l0), lo, hi)
    red_weights(l0, ends, lo + 1, hi - 1)
    black_weights(l0, ends, lo + 2, hi - 2)
    arrive([item for item in send_e0 if item[0] != 0])
    far_lo, far_hi = reach(l0, deep)
    pack(l0, lambda x: e0[x], put_e(l0), 0, lo)
    pack(l0, lambda x: e0[x], put_e(l0), hi, l0.pairs)
    red_weights(l0, ends, far_lo - 1, lo + 1)
    red_weights(l0, ends, hi - 1, far_hi + 1)
    black_weights(l0, ends, far_lo, lo + 2)
    black_weights(l0, ends, hi - 2, far_hi)
    arrive(send_f0)
    start(l0, lambda x: f0[x], deep - 1, deep)
    sweeps(l0, SMOOTH - 1, 1)
    go(send_v0)
    residual_sums(l0, tmp)
    f1[pl.ds(l1.rim_x, l1.block_x), pl.ds(l1.rim_y, l1.block_y), :] = restrict(
        tmp, l1.block_x, l0.block_y
    )
    go(send_f1)

    arrive(send_e1)
    pack(l1, lambda x: e1[x], put_e(l1), 0, l1.pairs)
    coefficients(l1, deep)
    arrive(send_f1)
    start(l1, lambda x: f1[x], deep - 1, deep + 1)
    sweeps(l1, SMOOTH - 1, 1)
    go(send_v1)
    residual_sums(l1, tmp)
    gather_start(1, restrict(tmp, block2, l1.block_y))

    full, big = refs["full"], refs["big"]
    full[...] = jnp.zeros(full.shape, F32)
    gather_wait(0, full)
    pack(l2, lambda x: full[x, 8 : 8 + l2.high], put_e(l2), 0, l2.pairs)
    for fine, coarse in ((l2, l3), (l3, l4)):
        for c in range(2):
            wrap(fine, fine.e[c])
        coefficients(fine, 0)
        for t in range(fine.pairs):
            put_rows(big, t, fine.e[0][t + 1] + fine.e[1][t + 1])
        rows = narrow(restrict(big, fine.pairs, fine.high), gx * coarse.zlen, 1.0)
        coarse.full[...] = rows
        pack(coarse, lambda x: coarse.full[x], put_e(coarse), 0, coarse.pairs)
    for c in range(2):
        wrap(l4, l4.e[c])
    coefficients(l4, 0)

    gather_wait(1, full)
    start(l2, lambda x: full[x, 8 : 8 + l2.high], 0, 0)
    sweeps(l2, SMOOTH - 1, 0)
    for fine, coarse in ((l2, l3), (l3, l4)):
        residual_sums(fine, big)
        coarse.full[...] = restrict(big, fine.pairs, fine.high)
        small = coarse is l4 and coarse.pairs == 1
        start(coarse, lambda x: coarse.full[x], None if small else 0, 0)
        if small:
            solve_small(coarse, COARSE_SWEEPS)
        else:
            sweeps(coarse, SMOOTH - 1 if coarse is l3 else COARSE_SWEEPS - 1, 0)

    def correct(fine, coarse):
        s = even_mask(coarse.high, coarse.lanes)
        spread(big, jnp.stack([coarse_row(coarse, s, t) for t in range(fine.pairs)]))
        for c in range(2):
            for t in range(fine.pairs):
                fine.v[c][t + 1] = fine.v[c][t + 1] + get_row(big, t, fine.high)
            wrap(fine, fine.v[c])
        sweeps(fine, SMOOTH, 0)

    correct(l3, l4)
    correct(l2, l3)

    def add(level, halo, far_lo, far_hi):
        lo, hi = reach(level, 0)
        ylo, yhi = level.rim_y, level.rim_y + level.block_y
        for c in range(2):
            for t in list(range(far_lo, lo)) + list(range(hi, far_hi)):
                level.v[c][t + 1] = halo[c, t + 1] + get_row(tmp, t - far_lo, level.high)

            def step(t):
                row = jnp.concatenate(
                    [
                        halo[c, t + 1, 0:ylo],
                        level.v[c][t + 1, ylo:yhi],
                        halo[c, t + 1, yhi : level.high],
                    ],
                    axis=0,
                )
                level.v[c][t + 1] = row + get_row(tmp, t - far_lo, level.high)

            loop(level, lo, hi, step)

    s2 = even_mask(l2.high, l2.lanes)
    for x in range(block2):
        full[x, 8 : 8 + l2.high, :] = coarse_row(l2, s2, x)
    rows = []
    high = l1.high // 2
    skip = 8 - l1.rim_y // 2
    for t in range(l1.pairs):
        x = t - l1.rim_pairs
        p = lax.rem(me_x + x // block2 + gx, gx)
        value = full[x % block2, pl.ds(pl.multiple_of(me_y * 8, 8), 24), :]
        value = pltpu.roll(value, lax.rem(l2.lanes - p * z2, l2.lanes), 1)
        rows.append(value[skip : skip + high, 0:128])
    arrive(send_v1)
    sent(send_v1)
    spread(tmp, jnp.stack(rows))
    add(l1, vh1, 0, l1.pairs)
    sweeps(l1, SMOOTH, 2)

    s1 = even_mask(l1.high, l1.lanes)
    first = l1.rim_x - l0.rim_pairs
    low = l1.rim_y - l0.rim_y // 2
    far_lo, far_hi = reach(l0, deep)
    rows = [coarse_row(l1, s1, first + t)[low : low + l0.high // 2] for t in range(far_lo, far_hi)]
    arrive(send_v0)
    sent(send_v0)
    spread(tmp, jnp.stack(rows))
    add(l0, vh0, far_lo, far_hi)
    sweeps(l0, SMOOTH, 0)

    s0 = even_mask(l0.high, l0.lanes)

    def last(t):
        red, black = l0.v[0][t + l0.rim_pairs + 1], l0.v[1][t + l0.rim_pairs + 1]
        lo, hi = l0.rim_y, l0.rim_y + l0.block_y
        out_ref[2 * t] = jnp.where(s0, red, black)[lo:hi]
        out_ref[2 * t + 1] = jnp.where(s0, black, red)[lo:hi]

    loop(l0, 0, l0.block_pairs, last)
    for group in (send_e0, send_f0, send_e1, send_f1):
        sent(group)
    for kind in range(2):
        gather_end(kind)


def per_device(gx, gy, right_side, permittivity):
    bx, by, nz = right_side.shape
    n = gx * gy
    wide = -(-gx * (nz // 4) // 128) * 128
    scratch, names = [], []

    def buffer(owner, name, *shape):
        scratch.append(pltpu.VMEM(shape, F32))
        names.append((owner, name))

    refs = {}
    levels = []
    for index in range(LEVELS):
        level = Level()
        level.index, level.gx = index, gx
        level.zlen = nz >> index
        level.whole = index >= 2
        level.block_x = bx >> index
        if level.whole:
            level.rim_x = level.rim_y = level.rim_pairs = 0
            level.pairs = level.block_pairs = level.block_x // 2
            level.high = level.block_y = (by >> index) * gy
            level.lanes = wide
        else:
            level.rim_x, level.rim_y = 6, 8
            level.block_y = by >> index
            level.rim_pairs, level.block_pairs = level.rim_x // 2, level.block_x // 2
            level.pairs = level.block_pairs + 2 * level.rim_pairs
            level.high = level.block_y + 2 * level.rim_y
            level.lanes = nz
        size = (level.high, level.lanes)
        level.e, level.v = [None, None], [None, None]
        for c in range(2):
            buffer(level.e, c, level.pairs + 2, *size)
            buffer(level.v, c, level.pairs + 2, *size)
        buffer(level, "inv", 2, level.pairs, *size)
        buffer(level, "a", 2, 6, level.pairs, *size)
        if index < 2:
            buffer(None, f"e{index}", 2 * level.pairs, *size)
            buffer(None, f"f{index}", 2 * level.pairs, *size)
            buffer(None, f"vh{index}", 2, level.pairs + 2, *size)
        if index == 2:
            buffer(None, "big", level.pairs, level.lanes // 128, level.high, 128)
            buffer(None, "full", level.block_x, level.high + 16, level.lanes)
        if index > 2:
            buffer(level, "full", level.block_x, *size)
        levels.append(level)
    l0 = levels[0]
    buffer(None, "tmp", l0.pairs, 1, l0.high, l0.lanes)
    groups = levels[2].block_x // (128 // levels[2].zlen)
    buffer(None, "stage", 2, n, groups, 8, 128)
    buffer(None, "packed", 2, groups, 8, 128)
    sems = [
        pltpu.SemaphoreType.DMA((8, 8)),
        pltpu.SemaphoreType.DMA((8, 8)),
        pltpu.SemaphoreType.DMA((2,)),
        pltpu.SemaphoreType.DMA((2,)),
    ]

    def body(right_ref, permit_ref, out_ref, *buffers):
        me_x, me_y = lax.axis_index("gx"), lax.axis_index("gy")
        for (owner, name), ref in zip(names, buffers):
            if owner is None:
                refs[name] = ref
            elif isinstance(owner, list):
                owner[name] = ref
            else:
                setattr(owner, name, ref)
        refs["sems"] = buffers[len(names) :]
        for level in levels:
            if level.whole:
                level.first_x, level.last_x = 0, level.pairs - 1
                level.first_y, level.last_y = 0, level.high - 1
            else:
                level.first_x = level.rim_pairs - me_x * level.block_pairs
                level.last_x = level.first_x + gx * level.block_pairs - 1
                level.first_y = level.rim_y - me_y * level.block_y
                level.last_y = level.first_y + gy * level.block_y - 1
        kernel(gx, gy, right_ref, permit_ref, out_ref, refs, levels)

    return pl.pallas_call(
        body,
        out_shape=jax.ShapeDtypeStruct(right_side.shape, F32),
        in_specs=[pl.BlockSpec(memory_space=pltpu.VMEM)] * 2,
        out_specs=pl.BlockSpec(memory_space=pltpu.VMEM),
        scratch_shapes=scratch + sems,
        compiler_params=pltpu.CompilerParams(
            collective_id=0, has_side_effects=True, vmem_limit_bytes=60 * 2**20
        ),
    )(right_side, permittivity)


def solution(mesh):
    gx, gy = mesh.shape["gx"], mesh.shape["gy"]
    placed = (P("gx", "gy", None), P("gx", "gy", None))
    return jax.shard_map(
        functools.partial(per_device, gx, gy),
        mesh=mesh,
        in_specs=placed,
        out_specs=P("gx", "gy", None),
        check_vma=False,
    )
```

profile of v0, /device:TPU:1, one launch (start us, length us, event | category | flops | bytes accessed | tf_op | source)
XLA Modules:
  0.0 48.3 jit_solution(14421354591792994588)
XLA Ops:
  0.0 46.4 %shard_map.28 = f32[32,32,128]{2,1,0:T(8,128)} custom-call(f32[32,32,128]{2,1,0:T(8,128)} %right_ref.1, f32[32,32,128]{2,1,0:T(8,128)} %permit_ref.1), custom_call_target="tpu_custom_call" | custom-call | tf_op jit(solution)/shard_map/pallas_call | solution.py:711
  46.4 1.9 %copy.4 = f32[32,32,128]{2,1,0:T(8,128)} copy(f32[32,32,128]{2,1,0:T(8,128)} %shard_map.28) | data formatting | bytes 1048576
where the time goes:
time: 48.8 us; the launch traced here: 48.3 us
  Pallas kernels  46.4 us (95%)
  local copies, waits for them, and re-layouts  1.87 us (4%)
    pallas_call x1, Pallas kernels, per_device(): pl.pallas_call(body, out_shape=jax.ShapeDtypeStruct(right_side.shape, F32...  46.4 us
    unnamed x1, local copies, waits for them, and re-layouts  1.87 us

commit v1 on v0

--- a/solution.py
+++ b/solution.py
@@ -309,10 +309,8 @@
 
 def kernel(gx, gy, right_ref, permit_ref, out_ref, refs, lv):
     me_x, me_y = lax.axis_index("gx"), lax.axis_index("gy")
-    me = me_x * gy + me_y
-    n = gx * gy
     l0, l1, l2, l3, l4 = lv
-    send_sem, recv_sem, all_send, all_recv = refs["sems"]
+    send_sem, recv_sem, all_send, all_recv, local = refs["sems"]
 
     def inside(dx, dy):
         x, y = me_x + dx, me_y + dy
@@ -368,6 +366,12 @@
         send_v0 += copies(4 + c, l0.v[c], vh0.at[c], deep // 2, p0)
         send_v1 += copies(6 + c, l1.v[c], vh1.at[c], deep // 2 + 1, p1)
 
+    x0, y0 = pl.ds(l0.rim_x, l0.block_x), pl.ds(l0.rim_y, l0.block_y)
+    load_e = pltpu.make_async_copy(permit_ref, e0.at[x0, y0, :], local.at[0])
+    load_f = pltpu.make_async_copy(right_ref, f0.at[x0, y0, :], local.at[1])
+    load_e.start()
+    load_f.start()
+
     def fill(ref, lead, value, geometry):
         rim_x, block_x, rim_y, block_y = geometry
         rows, high, width = ref.shape[-3:]
@@ -388,30 +392,45 @@
     for c in range(2):
         fill(vh0, (c,), 0.0, p0)
         fill(vh1, (c,), 0.0, p1)
-    x0, y0 = pl.ds(l0.rim_x, l0.block_x), pl.ds(l0.rim_y, l0.block_y)
-    e0[x0, y0, :] = permit_ref[...]
-    f0[x0, y0, :] = right_ref[...]
-
     barrier = pltpu.get_barrier_semaphore()
 
-    def device(d):
-        t = lax.rem(me + d, n)
-        return (lax.div(t, gy), lax.rem(t, gy))
-
-    def greet(d, _):
-        pl.semaphore_signal(barrier, inc=1, device_id=device(d), device_id_type=MESH)
-        return 0
-
-    lax.fori_loop(1, n, greet, 0)
+    def in_x(d):
+        return (lax.rem(me_x + d, gx), me_y)
+
+    def in_y(d):
+        return (me_x, lax.rem(me_y + d, gy))
+
+    def greet(to, count):
+        def step(d, carry):
+            pl.semaphore_signal(barrier, inc=1, device_id=to(d), device_id_type=MESH)
+            return carry
+
+        lax.fori_loop(1, count, step, 0)
+
+    greet(in_x, gx)
+    greet(in_y, gy)
+    guests = jnp.int32(gx - 1 + gy - 1)
+    for dx, dy in DIRS:
+        if dx != 0 and dy != 0:
+
+            @pl.when(inside(dx, dy))
+            def _():
+                pl.semaphore_signal(
+                    barrier, inc=1, device_id=(me_x + dx, me_y + dy), device_id_type=MESH
+                )
+
+            guests = guests + inside(dx, dy).astype(jnp.int32)
     for level in (l0, l1):
         for c in range(2):
             for t in list(range(3)) + list(range(level.pairs - 1, level.pairs + 2)):
                 level.v[c][t] = jnp.zeros((level.high, level.lanes), F32)
             for t in (0, level.pairs + 1):
                 level.e[c][t] = jnp.ones((level.high, level.lanes), F32)
-    pl.semaphore_wait(barrier, n - 1)
-
+    pl.semaphore_wait(barrier, guests)
+
+    load_e.wait()
     go(send_e0)
+    load_f.wait()
     go(send_f0)
 
     tmp = refs["tmp"]
@@ -424,11 +443,10 @@
     put_rows(
         tmp,
         pl.ds(0, l1.block_x),
-        permit_ref[...].reshape(l1.block_x, 2, l0.block_y, lanes).sum(axis=1),
+        e0[x0, y0, :].reshape(l1.block_x, 2, l0.block_y, lanes).sum(axis=1),
     )
     own_e1 = narrow(restrict(tmp, l1.block_x, l0.block_y), l1.zlen, 1.0)
     e1[pl.ds(l1.rim_x, l1.block_x), pl.ds(l1.rim_y, l1.block_y), :] = own_e1
-    go(send_e1)
 
     block2, z2 = l2.block_x, l2.zlen
     per = 128 // z2
@@ -442,25 +460,34 @@
             for k in range(1, per):
                 value = jnp.where(group == k, roll(rows[g * per + k], k * z2, 1), value)
             packed[g] = value
-            stage[me, g] = value
-
-        def step(d, _):
+            stage[me_y, me_x, g] = value
+
+        gather_line(kind, 0, in_x, gx, packed, stage.at[me_y, me_x])
+
+    def gather_line(kind, stop, to, count, src, dst):
+        def step(d, carry):
             pltpu.make_async_remote_copy(
-                src_ref=packed,
-                dst_ref=stage.at[me],
-                send_sem=all_send.at[kind],
-                recv_sem=all_recv.at[kind],
-                device_id=device(d),
+                src_ref=src,
+                dst_ref=dst,
+                send_sem=all_send.at[kind, stop],
+                recv_sem=all_recv.at[kind, stop],
+                device_id=to(d),
                 device_id_type=MESH,
             ).start()
-            return 0
-
-        lax.fori_loop(1, n, step, 0)
+            return carry
+
+        lax.fori_loop(1, count, step, 0)
+
+    def gather_next(kind):
+        stage = refs["stage"].at[kind]
+        others = stage.at[me_y, pl.ds(0, gx - 1)]
+        pltpu.make_async_copy(others, others, all_recv.at[kind, 0]).wait()
+        gather_line(kind, 1, in_y, gy, stage.at[me_y], stage.at[me_y])
 
     def gather_wait(kind, full):
         stage = refs["stage"].at[kind]
-        others = stage.at[pl.ds(0, n - 1)]
-        pltpu.make_async_copy(others, others, all_recv.at[kind]).wait()
+        others = stage.at[pl.ds(0, gy - 1)]
+        pltpu.make_async_copy(others, others, all_recv.at[kind, 1]).wait()
         group = iota((8, 128), 1) // z2
 
         def step(q, _):
@@ -472,7 +499,7 @@
                         p = h * per + k
                         if p >= gx:
                             break
-                        part = roll(stage[p * gy + q, x // per], (k - x % per) * z2, 1)
+                        part = roll(stage[q, p, x // per], (k - x % per) * z2, 1)
                         value = part if k == 0 else jnp.where(group == k, part, value)
                     tiles.append(value)
                 row = tiles[0] if len(tiles) == 1 else jnp.concatenate(tiles, axis=1)
@@ -482,11 +509,13 @@
         lax.fori_loop(0, gy, step, 0)
 
     def gather_end(kind):
-        others = refs["stage"].at[kind, pl.ds(0, n - 1)]
-        pltpu.make_async_copy(others, others, all_send.at[kind]).wait()
+        others = refs["stage"].at[kind, 0, pl.ds(0, gx - 1)]
+        pltpu.make_async_copy(others, others, all_send.at[kind, 0]).wait()
+        others = refs["stage"].at[kind, pl.ds(0, gy - 1)]
+        pltpu.make_async_copy(others, others, all_send.at[kind, 1]).wait()
 
     put_rows(tmp, pl.ds(0, block2), own_e1.reshape(block2, 2, l1.block_y, lanes).sum(axis=1))
-    gather_start(0, restrict(tmp, block2, l1.block_y))
+    own_e2 = restrict(tmp, block2, l1.block_y)
 
     arrive([item for item in send_e0 if item[0] == 0])
     lo, hi = reach(l0, 0)
@@ -495,6 +524,8 @@
     red_weights(l0, ends, lo + 1, hi - 1)
     black_weights(l0, ends, lo + 2, hi - 2)
     arrive([item for item in send_e0 if item[0] != 0])
+    gather_start(0, own_e2)
+    go(send_e1)
     far_lo, far_hi = reach(l0, deep)
     pack(l0, lambda x: e0[x], put_e(l0), 0, lo)
     pack(l0, lambda x: e0[x], put_e(l0), hi, l0.pairs)
@@ -505,12 +536,12 @@
     arrive(send_f0)
     start(l0, lambda x: f0[x], deep - 1, deep)
     sweeps(l0, SMOOTH - 1, 1)
-    go(send_v0)
     residual_sums(l0, tmp)
     f1[pl.ds(l1.rim_x, l1.block_x), pl.ds(l1.rim_y, l1.block_y), :] = restrict(
         tmp, l1.block_x, l0.block_y
     )
     go(send_f1)
+    gather_next(0)
 
     arrive(send_e1)
     pack(l1, lambda x: e1[x], put_e(l1), 0, l1.pairs)
@@ -518,13 +549,13 @@
     arrive(send_f1)
     start(l1, lambda x: f1[x], deep - 1, deep + 1)
     sweeps(l1, SMOOTH - 1, 1)
-    go(send_v1)
     residual_sums(l1, tmp)
     gather_start(1, restrict(tmp, block2, l1.block_y))
 
     full, big = refs["full"], refs["big"]
     full[...] = jnp.zeros(full.shape, F32)
     gather_wait(0, full)
+    gather_next(1)
     pack(l2, lambda x: full[x, 8 : 8 + l2.high], put_e(l2), 0, l2.pairs)
     for fine, coarse in ((l2, l3), (l3, l4)):
         for c in range(2):
@@ -540,6 +571,8 @@
     coefficients(l4, 0)
 
     gather_wait(1, full)
+    go(send_v1)
+    go(send_v0)
     start(l2, lambda x: full[x, 8 : 8 + l2.high], 0, 0)
     sweeps(l2, SMOOTH - 1, 0)
     for fine, coarse in ((l2, l3), (l3, l4)):
@@ -630,7 +663,6 @@
 
 def per_device(gx, gy, right_side, permittivity):
     bx, by, nz = right_side.shape
-    n = gx * gy
     wide = -(-gx * (nz // 4) // 128) * 128
     scratch, names = [], []
 
@@ -678,12 +710,13 @@
     l0 = levels[0]
     buffer(None, "tmp", l0.pairs, 1, l0.high, l0.lanes)
     groups = levels[2].block_x // (128 // levels[2].zlen)
-    buffer(None, "stage", 2, n, groups, 8, 128)
+    buffer(None, "stage", 2, gy, gx, groups, 8, 128)
     buffer(None, "packed", 2, groups, 8, 128)
     sems = [
         pltpu.SemaphoreType.DMA((8, 8)),
         pltpu.SemaphoreType.DMA((8, 8)),
-        pltpu.SemaphoreType.DMA((2,)),
+        pltpu.SemaphoreType.DMA((2, 2)),
+        pltpu.SemaphoreType.DMA((2, 2)),
         pltpu.SemaphoreType.DMA((2,)),
     ]
 
@@ -711,7 +744,7 @@
     return pl.pallas_call(
         body,
         out_shape=jax.ShapeDtypeStruct(right_side.shape, F32),
-        in_specs=[pl.BlockSpec(memory_space=pltpu.VMEM)] * 2,
+        in_specs=[pl.BlockSpec(memory_space=pl.ANY)] * 2,
         out_specs=pl.BlockSpec(memory_space=pltpu.VMEM),
         scratch_shapes=scratch + sems,
         compiler_params=pltpu.CompilerParams(

time: 48.8 us -> 45.3 us (0.928)
  Pallas kernels: 46.4 us -> 43.2 us
    pallas_call x1, Pallas kernels: 46.4 us -> 43.2 us  [per_device(): pl.pallas_call(body, out_shape=jax.ShapeDtypeStruct(right_side.shape, F32...]
where the time goes in v1:
time: 45.3 us; the launch traced here: 45.1 us
  Pallas kernels  43.2 us (95%)
  local copies, waits for them, and re-layouts  1.87 us (4%)
    pallas_call x1, Pallas kernels, per_device(): pl.pallas_call(body, out_shape=jax.ShapeDtypeStruct(right_side.shape, F32...  43.2 us
    unnamed x1, local copies, waits for them, and re-layouts  1.87 us

profile of v1, /device:TPU:1, one launch (start us, length us, event | category | flops | bytes accessed | tf_op | source)
XLA Modules:
  0.0 45.1 jit_solution(14249650594900594036)
XLA Ops:
  0.0 43.2 %shard_map.28 = f32[32,32,128]{2,1,0:T(8,128)} custom-call(f32[32,32,128]{2,1,0:T(8,128)} %right_ref.1, f32[32,32,128]{2,1,0:T(8,128)} %permit_ref.1), custom_call_target="tpu_custom_call" | custom-call | tf_op jit(solution)/shard_map/pallas_call | solution.py:744
  43.2 1.9 %copy.4 = f32[32,32,128]{2,1,0:T(8,128)} copy(f32[32,32,128]{2,1,0:T(8,128)} %shard_map.28) | data formatting | bytes 1048576
